TPU v7x, 256 devices: a whole 4x4x8 slice. The times are simulated.
256 devices in a mesh: rows: 128 (over y, z, x), rep: 2 (over core).
Axes of the slice: x: 4, y: 4, z: 8, core: 2. Of those that a mesh axis runs over, the one named last changes fastest.
Arguments:
- features: bfloat16 [131072, 128], P('rows'), may hold values from -6 to 6
- weight: bfloat16 [128, 256], replicated, may hold values from -0.5 to 0.5
- tiles: bfloat16 [1024, 64, 128, 128], P('rows', 'rep'), may hold values from -0.0625 to 0.0625
- tile_cols: int32 [1024, 64], P('rows', 'rep'), may hold values from 0 to 1023, as said below
- order: int32 [1024], replicated, may hold values from 0 to 1023, as said below
- cotangent: bfloat16 [131072, 256], P('rows'), may hold values from -24 to 24
Outputs:
- activated: bfloat16 [131072, 256], P('rows')
- feature_grad: float32 [131072, 128], P('rows')
- weight_grad: float32 [128, 256], replicated
Inputs may be any that keep to these rules, and one draw needn't show every extreme that they name: `tile_cols`: the 64 column tiles of one tile row are all different. Among the 32 slots of the 8 tile rows that one index of rows and one index of rep hold, exactly 2 name (through order) blocks owned by each index of rows, that is blocks o * 8 to (o + 1) * 8 - 1 for index o; all blocks named by the slots of one index of rows are different. `order`: A permutation of the tile rows.
All inputs are finite; a program needn't handle non-finite values.
Results may differ from a plain program's by a relative error of at most 0.0055.
Values may be sent and summed in bfloat16 or wider, within the bound.
No kernel may reach another device: no remote copies, remote signals or barrier semaphores. Data moves between devices by JAX's collectives and lax.ppermute only.
A program may use at most 192 MiB of HBM per device.

v0:
```python
import jax
import jax.numpy as jnp
from jax import lax
from jax.sharding import PartitionSpec as P


def body(features, weight, tiles, tile_cols, order, cotangent):
    tile_rows = tiles.shape[0]
    row_slots = tiles.shape[1]
    side = tiles.shape[2]
    width = features.shape[1]
    n_tiles = order.shape[0]
    senders = lax.axis_size("rows")
    copies = lax.axis_size("rep")
    core = lax.axis_index("rep")
    slots = tile_rows * row_slots
    per_owner = slots // senders
    own_rows = features.shape[0]
    half = own_rows // copies
    offset = core * half
    labels = jnp.arange(n_tiles, dtype=jnp.int32)
    flat_cols = tile_cols.reshape(-1)
    block = jnp.sum(jnp.where(flat_cols[:, None] == labels[None, :], order[None, :], 0), axis=1)
    owner = block // tile_rows
    local_block = block % tile_rows
    owner_hits = (owner[:, None] == jnp.arange(senders, dtype=jnp.int32)[None, :]).astype(jnp.int32)
    before = jnp.cumsum(owner_hits, axis=0) - owner_hits
    rank = jnp.sum(before * owner_hits, axis=1)
    position = owner * per_owner + rank
    slot_ids = jnp.arange(slots, dtype=jnp.int32)
    match = position[None, :] == slot_ids[:, None]
    wanted = jnp.sum(jnp.where(match, local_block[None, :], 0), axis=1)
    slot_of = jnp.sum(jnp.where(match, slot_ids[None, :], 0), axis=1)
    incoming = lax.all_to_all(
        wanted.reshape(senders, per_owner), "rows", split_axis=0, concat_axis=0, tiled=True
    )
    feature_blocks = features.reshape(tile_rows, side, width)
    replies = feature_blocks[incoming]
    arrived = lax.all_to_all(replies, "rows", split_axis=0, concat_axis=0, tiled=True).reshape(
        slots, side, width
    )
    picked = arrived[position].reshape(tile_rows, row_slots, side, width)
    local_sum = jnp.einsum("bkij,bkjf->bif", tiles, picked, preferred_element_type=jnp.float32)
    summed = lax.psum(local_sum.reshape(own_rows, width), "rep")
    aggregated = summed.astype(jnp.bfloat16)
    pre = jnp.dot(aggregated, weight, preferred_element_type=jnp.float32)
    sig = jax.nn.sigmoid(pre)
    activated = (pre * sig).astype(jnp.bfloat16)
    pre_grad = (cotangent.astype(jnp.float32) * sig * (1.0 + pre * (1.0 - sig))).astype(
        jnp.bfloat16
    )
    agg_half = lax.dynamic_slice_in_dim(aggregated, offset, half, 0)
    grad_half = lax.dynamic_slice_in_dim(pre_grad, offset, half, 0)
    local_weight = jnp.dot(agg_half.T, grad_half, preferred_element_type=jnp.float32)
    weight_grad = lax.psum(local_weight, ("rows", "rep"))
    spread = jnp.dot(pre_grad, weight.T, preferred_element_type=jnp.float32).astype(jnp.bfloat16)
    spread_blocks = spread.reshape(tile_rows, side, width)
    terms = jnp.einsum("bkij,bif->bkjf", tiles, spread_blocks, preferred_element_type=jnp.float32)
    outgoing = terms.reshape(slots, side, width)[slot_of]
    targets = jnp.arange(tile_rows, dtype=jnp.int32)
    received = lax.all_to_all(
        outgoing.reshape(senders, per_owner, side, width),
        "rows",
        split_axis=0,
        concat_axis=0,
        tiled=True,
    )
    selector = (incoming.reshape(-1)[None, :] == targets[:, None]).astype(jnp.float32)
    owned = jnp.dot(
        selector, received.reshape(slots, side * width), precision=lax.Precision.HIGHEST
    )
    feature_grad = lax.psum(owned.reshape(own_rows, width), "rep")
    return (activated, feature_grad, weight_grad)


def solution(mesh):
    in_specs = (
        P("rows", None),
        P(),
        P("rows", "rep", None, None),
        P("rows", "rep"),
        P(),
        P("rows", None),
    )
    out_specs = (P("rows", None), P("rows", None), P())
    return jax.shard_map(body, mesh=mesh, in_specs=in_specs, out_specs=out_specs, check_vma=False)
```

profile of v0, /device:TPU:1, one launch (start us, length us, event | category | flops | bytes accessed | tf_op | source)
XLA Modules:
  0.0 762.1 jit_solution(630971453472746934)
XLA Ops:
  7.2 0.0 copy-start
  7.2 0.8 eq.66
  8.0 1.0 select_reduce_fusion
  9.0 0.1 copy.19
  9.1 0.2 fusion.5
  9.4 0.2 fusion.7
  9.6 0.2 select_reduce_fusion.1
  9.8 0.1 all_to_all.14
  9.9 26.7 %all_to_all.22 = s32[128,1,2]{2,1,0:T(1,128)S(1)} all-to-all(s32[128,1,2]{2,1,0:T(1,128)S(1)} %bitcast.72), channel_id=1, replica_groups=mesh['rows'=128,'rep'=2] {'rows'}, dimensions={0} | all-to-all | bytes 2048 | tf_op jit(solution)/shard_map/all_to_all | solution.py:34
  36.6 0.1 reshape.215
  36.8 0.0 copy-done
  36.8 8.6 %gather_fusion = bf16[256,128,128]{2,1,0:T(8,128)(2,1)} fusion(bf16[8,128,128]{2,1,0:T(8,128)(2,1)S(1)} %bitcast.62, s32[1024]{0:T(1024)S(1)} %pad_clamp_fusion.2), kind=kCustom, calls=%fused_computation | custom fusion | bytes 16778240 | tf_op jit(solution)/shard_map/gather | solution.py:38
  45.4 7.7 %all-to-all-start.1 = ((bf16[128,2,128,128]{3,2,1,0:T(8,128)(2,1)}), bf16[128,2,128,128]{3,2,1,0:T(8,128)(2,1)}, u32[]{:S(2)}, u32[]{:S(2)}) async-start(bf16[128,2,128,128]{3,2,1,0:T(8,128)(2,1)} %bitcast.65), calls=%async_computation.1 | async-start | bytes 16777216 | tf_op jit(solution)/shard_map/all_to_all | solution.py:39
  53.1 183.2 %all-to-all-done.1 = bf16[128,2,128,128]{3,2,1,0:T(8,128)(2,1)} async-done(((bf16[128,2,128,128]{3,2,1,0:T(8,128)(2,1)}), bf16[128,2,128,128]{3,2,1,0:T(8,128)(2,1)}, u32[]{:S(2)}, u32[]{:S(2)}) %all-to-all-start.1) | async-done | bytes 8388640 | tf_op jit(solution)/shard_map/all_to_all | solution.py:39
  236.3 12.0 %gather_fusion.1 = bf16[256,128,128]{2,1,0:T(8,128)(2,1)} fusion(bf16[256,128,128]{2,1,0:T(8,128)(2,1)} %bitcast.8, s32[1024]{0:T(1024)S(1)} %pad_clamp_fusion.1), kind=kCustom, calls=%fused_computation.1 | custom fusion | bytes 16778240 | tf_op jit(solution)/shard_map/gather | solution.py:42
  248.3 0.0 copy-start.2
  248.3 0.0 copy-start.3
  248.3 8.2 %fusion.14 = f32[8,128,128,1]{1,2,3,0:T(8,128)S(1)} fusion(bf16[8,32,128,128]{3,2,1,0:T(8,128)(2,1)} %param.8, bf16[8,32,128,128]{3,2,1,0:T(8,128)(2,1)} %bitcast.66), kind=kOutput, calls=%fused_computation.55 | convolution fusion | flops 1073741824 | bytes 17301504 | tf_op jit(solution)/shard_map/bkij,bkjf->bif/dot_general | solution.py:43
  256.5 8.9 %all-reduce.7 = bf16[1024,128]{1,0:T(8,128)(2,1)S(1)} all-reduce(f32[1024,128]{1,0:T(8,128)S(1)} %bitcast.67), channel_id=1, replica_groups=mesh['rows'=128,'rep'=2] {'rep'}, use_global_device_ids=true, to_apply=%region_5.6 | all-reduce | flops 131072 | bytes 786432 | tf_op jit(solution)/shard_map/psum | solution.py:44
  265.4 0.0 copy-done.2
  265.4 0.0 copy-done.3
  265.4 1.4 multiply_convert_fusion
  266.9 0.3 convolution_convert_fusion
  267.1 11.5 %fusion.13 = f32[8,128,32,128]{3,1,2,0:T(8,128)} fusion(bf16[8,128,128,1]{2,1,3,0:T(8,128)(2,1)S(1)} %bitcast.68, bf16[8,32,128,128]{3,2,1,0:T(8,128)(2,1)} %param.8), kind=kOutput, calls=%fused_computation.54 | convolution fusion | flops 1073741824 | bytes 25427968 | tf_op jit(solution)/shard_map/bkij,bif->bkjf/dot_general | solution.py:58
  278.6 17.7 %gather_fusion.2 = f32[256,128,128]{1,2,0:T(8,128)} fusion(f32[256,128,128]{1,2,0:T(8,128)} %bitcast.63, s32[1024]{0:T(1024)S(1)} %pad_clamp_fusion), kind=kCustom, calls=%fused_computation.2 | custom fusion | bytes 33555456 | tf_op jit(solution)/shard_map/gather | solution.py:59
  296.3 17.5 %copy.23 = f32[256,128,128]{2,1,0:T(8,128)} copy(f32[256,128,128]{1,2,0:T(8,128)} %gather_fusion.2) | data formatting | bytes 33554432 | tf_op jit(solution)/shard_map/gather | solution.py:59
  313.7 7.8 %all-to-all-start.2 = ((f32[128,2,128,128]{3,2,1,0:T(8,128)}), f32[128,2,128,128]{3,2,1,0:T(8,128)}, u32[]{:S(2)}, u32[]{:S(2)}) async-start(f32[128,2,128,128]{3,2,1,0:T(8,128)} %bitcast.64), calls=%async_computation.2 | async-start | bytes 33554432 | tf_op jit(solution)/shard_map/all_to_all | solution.py:61
  321.5 0.0 all-reduce.6.cloned.1.call-start
  321.6 0.5 broadcast.254
  322.1 0.8 reduce.3
  322.9 0.1 eq.79
  323.1 0.9 fusion.3
  323.9 0.0 all-reduce.6.cloned.1.call-update
  324.0 0.0 all-reduce.4.cloned.1.call-start
  324.0 365.5 %all-to-all-done.2 = f32[128,2,128,128]{3,2,1,0:T(8,128)} async-done(((f32[128,2,128,128]{3,2,1,0:T(8,128)}), f32[128,2,128,128]{3,2,1,0:T(8,128)}, u32[]{:S(2)}, u32[]{:S(2)}) %all-to-all-start.2) | async-done | bytes 16777248 | tf_op jit(solution)/shard_map/all_to_all | solution.py:61
  689.6 0.0 copy-start.1
  689.6 19.9 %fusion = f32[8,16384]{1,0:T(8,128)S(1)} fusion(f32[32,8,128,128]{3,2,1,0:T(8,128)} %bitcast.33, s32[256]{0:T(256)S(1)} %eq.79), kind=kOutput, calls=%fused_computation.3 | convolution fusion | flops 402655232 | bytes 17302528 | tf_op jit(solution)/shard_map/dot_general | solution.py:69
  709.4 0.9 reshape.212
  710.3 0.0 all-reduce.4.cloned.1.call-update
  710.3 0.0 all-reduce.6.cloned.1.call-done
  710.4 41.4 %all-reduce.4.cloned.1.call-done = f32[1024,128]{1,0:T(8,128)} async-done(((f32[1024,128]{1,0:T(8,128)}), f32[1024,128]{1,0:T(8,128)}) %all-reduce.4.cloned.1.call-update) | async-done | bytes 524304 | tf_op jit(solution)/shard_map/psum | solution.py:72
  751.8 1.9 copy.37
  753.7 1.6 copy.38
  755.3 0.0 copy-done.1
  (15 shorter events, 0.1 us)
Async XLA Ops:
  7.2 29.6 %copy-start = (bf16[1024,128]{1,0:T(8,128)(2,1)S(1)}, bf16[1024,128]{1,0:T(8,128)(2,1)}, u32[]{:S(2)}) copy-start(bf16[1024,128]{1,0:T(8,128)(2,1)} %param.6) | copy-start | bytes 786436
  45.4 191.0 %all-to-all-start.1 = ((bf16[128,2,128,128]{3,2,1,0:T(8,128)(2,1)}), bf16[128,2,128,128]{3,2,1,0:T(8,128)(2,1)}, u32[]{:S(2)}, u32[]{:S(2)}) async-start(bf16[128,2,128,128]{3,2,1,0:T(8,128)(2,1)} %bitcast.65), calls=%async_computation.1 | async-start | bytes 16777216 | tf_op jit(solution)/shard_map/all_to_all | solution.py:39
  248.3 17.1 %copy-start.2 = (bf16[128,256]{1,0:T(8,128)(2,1)S(1)}, bf16[128,256]{1,0:T(8,128)(2,1)}, u32[]{:S(2)}) copy-start(bf16[128,256]{1,0:T(8,128)(2,1)} %param.7) | copy-start | bytes 196612
  248.3 17.1 %copy-start.3 = (bf16[1024,256]{1,0:T(8,128)(2,1)S(1)}, bf16[1024,256]{1,0:T(8,128)(2,1)}, u32[]{:S(2)}) copy-start(bf16[1024,256]{1,0:T(8,128)(2,1)} %param.11) | copy-start | bytes 1572868
  313.7 375.8 %all-to-all-start.2 = ((f32[128,2,128,128]{3,2,1,0:T(8,128)}), f32[128,2,128,128]{3,2,1,0:T(8,128)}, u32[]{:S(2)}, u32[]{:S(2)}) async-start(f32[128,2,128,128]{3,2,1,0:T(8,128)} %bitcast.64), calls=%async_computation.2 | async-start | bytes 33554432 | tf_op jit(solution)/shard_map/all_to_all | solution.py:61
  321.5 388.8 %all-reduce.6.cloned.1.call-start = ((), (), s32[]{:S(2)}) async-start(), calls=%async_computation.4 | async-start | bytes 262144 | tf_op jit(solution)/shard_map/psum | solution.py:55
  324.0 427.8 %all-reduce.4.cloned.1.call-start = ((), (), s32[]{:S(2)}) async-start(), calls=%async_computation.3 | async-start | bytes 1048576 | tf_op jit(solution)/shard_map/psum | solution.py:72
  689.6 65.7 %copy-start.1 = (bf16[1024,128]{1,0:T(8,128)(2,1)S(1)}, bf16[1024,128]{1,0:T(8,128)(2,1)}, u32[]{:S(2)}) copy-start(bf16[1024,128]{1,0:T(8,128)(2,1)} %param.6) | copy-start | bytes 786436
Sparse Core Ops, SparseCore 0:
  328.5 375.3 all-reduce.5
  710.5 41.3 all-reduce.3
where the time goes:
time: 763 us; the launch traced here: 762 us
  waiting for transfers between devices  590 us (77%)
  local copies, waits for them, and re-layouts  61.9 us (8%)
  matrix products  42.1 us (6%)
  blocking collectives  35.6 us (5%)
  starting transfers between devices  15.5 us (2%)
  between operations  14.2 us (2%)
    all_to_all x1, waiting for transfers between devices, body(): lax.all_to_all(outgoing.reshape(senders, per_owner, side, width), 'rows',...  366 us
    all_to_all x1, waiting for transfers between devices, body(): lax.all_to_all(replies, 'rows', split_axis=0, concat_axis=0, tiled=True)  183 us
    psum x1, waiting for transfers between devices, body(): feature_grad = lax.psum(owned.reshape(own_rows, width), 'rep')  41.4 us
    gather x2, local copies, waits for them, and re-layouts, body(): outgoing = terms.reshape(slots, side, width)[slot_of]  35.1 us
    all_to_all x1, blocking collectives, body(): lax.all_to_all(wanted.reshape(senders, per_owner), 'rows', split_axis=0,...  26.7 us
    dot_general x1, matrix products, body(): jnp.dot(selector, received.reshape(slots, side * width), precision=lax.Pr...  19.9 us
  transfers between devices with their start and end apart: 4, of which 3 were waited for; matrix products, arithmetic and copies ran while one was open for 3% of the time, Pallas kernels for 0%

commit v1 on v0

--- a/solution.py
+++ b/solution.py
@@ -69,7 +69,7 @@
     owned = jnp.dot(
         selector, received.reshape(slots, side * width), precision=lax.Precision.HIGHEST
     )
-    feature_grad = lax.psum(owned.reshape(own_rows, width), "rep")
+    feature_grad = jnp.sum(lax.all_gather(owned.reshape(own_rows, width), "rep"), axis=0)
     return (activated, feature_grad, weight_grad)
 
 

time: 763 us -> 976 us (1.28)
  waiting for transfers between devices: 590 us -> 801 us
    psum x1, waiting for transfers between devices: 0.02 us -> 230 us  [body(): weight_grad = lax.psum(local_weight, ('rows', 'rep'))]
    psum x1 -> x0, waiting for transfers between devices: 41.4 us -> none  [body(): feature_grad = lax.psum(owned.reshape(own_rows, width), 'rep')]
    all_gather x0 -> x1, waiting for transfers between devices: none -> 25.1 us  [body(): lax.all_gather(owned.reshape(own_rows, width), 'rep')]
  transfers between devices with their start and end apart: 4 -> 4, of which waited for: 3 -> 4; matrix products, arithmetic and copies ran while one was open for 3% -> 0% of each run, Pallas kernels for 0% -> 0%
where the time goes in v1:
time: 976 us; the launch traced here: 975 us
  waiting for transfers between devices  801 us (82%)
  local copies, waits for them, and re-layouts  60 us (6%)
  matrix products  42.1 us (4%)
  blocking collectives  35.6 us (4%)
  between operations  15.7 us (2%)
  starting transfers between devices  15.5 us (2%)
    all_to_all x1, waiting for transfers between devices, body(): lax.all_to_all(outgoing.reshape(senders, per_owner, side, width), 'rows',...  363 us
    psum x1, waiting for transfers between devices, body(): weight_grad = lax.psum(local_weight, ('rows', 'rep'))  230 us
    all_to_all x1, waiting for transfers between devices, body(): lax.all_to_all(replies, 'rows', split_axis=0, concat_axis=0, tiled=True)  183 us
    gather x2, local copies, waits for them, and re-layouts, body(): outgoing = terms.reshape(slots, side, width)[slot_of]  35.1 us
    all_to_all x1, blocking collectives, body(): lax.all_to_all(wanted.reshape(senders, per_owner), 'rows', split_axis=0,...  26.7 us
    all_gather x1, waiting for transfers between devices, body(): lax.all_gather(owned.reshape(own_rows, width), 'rep')  25.1 us
    dot_general x1, matrix products, body(): jnp.dot(selector, received.reshape(slots, side * width), precision=lax.Pr...  19.9 us
  transfers between devices with their start and end apart: 4, of which 4 were waited for; matrix products, arithmetic and copies ran while one was open for 0% of the time, Pallas kernels for 0%

profile of v1, /device:TPU:1, one launch (start us, length us, event | category | flops | bytes accessed | tf_op | source)
XLA Modules:
  0.0 974.9 jit_solution(1464741527012388221)
XLA Ops:
  8.0 0.0 copy-start
  8.0 0.8 eq.66
  8.8 1.0 select_reduce_fusion
  9.8 0.1 copy.19
  9.9 0.2 fusion.5
  10.2 0.2 fusion.7
  10.4 0.2 select_reduce_fusion.1
  10.6 0.1 all_to_all.14
  10.7 26.7 %all_to_all.22 = s32[128,1,2]{2,1,0:T(1,128)S(1)} all-to-all(s32[128,1,2]{2,1,0:T(1,128)S(1)} %bitcast.72), channel_id=1, replica_groups=mesh['rows'=128,'rep'=2] {'rows'}, dimensions={0} | all-to-all | bytes 2048 | tf_op jit(solution)/shard_map/all_to_all | solution.py:34
  37.5 0.1 reshape.211
  37.6 0.0 copy-done
  37.6 8.6 gather_fusion
  46.2 7.7 all-to-all-start.1
  53.9 183.2 %all-to-all-done.1 = bf16[128,2,128,128]{3,2,1,0:T(8,128)(2,1)} async-done(((bf16[128,2,128,128]{3,2,1,0:T(8,128)(2,1)}), bf16[128,2,128,128]{3,2,1,0:T(8,128)(2,1)}, u32[]{:S(2)}, u32[]{:S(2)}) %all-to-all-start.1) | async-done | bytes 8388640 | tf_op jit(solution)/shard_map/all_to_all | solution.py:39
  237.2 12.0 %gather_fusion.1 = bf16[256,128,128]{2,1,0:T(8,128)(2,1)} fusion(bf16[256,128,128]{2,1,0:T(8,128)(2,1)} %bitcast.8, s32[1024]{0:T(1024)S(1)} %pad_clamp_fusion.1), kind=kCustom, calls=%fused_computation.1 | custom fusion | bytes 16778240 | tf_op jit(solution)/shard_map/gather | solution.py:42
  249.2 0.0 copy-start.2
  249.2 0.0 copy-start.3
  249.2 8.2 fusion.14
  257.3 8.9 all-reduce.4
  266.2 0.0 copy-done.2
  266.2 0.0 copy-done.3
  266.2 1.4 multiply_convert_fusion
  267.7 0.3 convolution_convert_fusion
  268.0 11.5 %fusion.13 = f32[8,128,32,128]{3,1,2,0:T(8,128)} fusion(bf16[8,128,128,1]{2,1,3,0:T(8,128)(2,1)S(1)} %bitcast.68, bf16[8,32,128,128]{3,2,1,0:T(8,128)(2,1)} %param.8), kind=kOutput, calls=%fused_computation.54 | convolution fusion | flops 1073741824 | bytes 25427968 | tf_op jit(solution)/shard_map/bkij,bif->bkjf/dot_general | solution.py:58
  279.4 17.7 %gather_fusion.2 = f32[256,128,128]{1,2,0:T(8,128)} fusion(f32[256,128,128]{1,2,0:T(8,128)} %bitcast.63, s32[1024]{0:T(1024)S(1)} %pad_clamp_fusion), kind=kCustom, calls=%fused_computation.2 | custom fusion | bytes 33555456 | tf_op jit(solution)/shard_map/gather | solution.py:59
  297.1 17.5 %copy.23 = f32[256,128,128]{2,1,0:T(8,128)} copy(f32[256,128,128]{1,2,0:T(8,128)} %gather_fusion.2) | data formatting | bytes 33554432 | tf_op jit(solution)/shard_map/gather | solution.py:59
  314.6 7.8 all-to-all-start.2
  322.4 0.0 all-gather.2.cloned.1.call-start
  322.4 0.5 broadcast.254
  322.9 0.8 reduce.3
  323.8 0.1 eq.79
  323.9 363.4 %all-to-all-done.2 = f32[128,2,128,128]{3,2,1,0:T(8,128)} async-done(((f32[128,2,128,128]{3,2,1,0:T(8,128)}), f32[128,2,128,128]{3,2,1,0:T(8,128)}, u32[]{:S(2)}, u32[]{:S(2)}) %all-to-all-start.2) | async-done | bytes 16777248 | tf_op jit(solution)/shard_map/all_to_all | solution.py:61
  687.3 0.0 copy-start.1
  687.3 19.9 %fusion = f32[8,16384]{1,0:T(8,128)S(1)} fusion(f32[32,8,128,128]{3,2,1,0:T(8,128)} %bitcast.33, s32[256]{0:T(256)S(1)} %eq.79), kind=kOutput, calls=%fused_computation.3 | convolution fusion | flops 402655232 | bytes 17302528 | tf_op jit(solution)/shard_map/dot_general | solution.py:69
  707.2 0.9 all_gather_reshape.3
  708.1 0.0 all-gather.2.cloned.1.call-update
  708.1 0.0 all-reduce.3.cloned.1.call-start
  708.2 0.9 fusion.3
  709.1 0.0 all-reduce.3.cloned.1.call-update
  709.1 25.1 %all-gather.2.cloned.1.call-done = f32[2,1024,128]{2,1,0:T(8,128)} async-done(((f32[1,1024,128]{2,1,0:T(8,128)}), f32[2,1024,128]{2,1,0:T(8,128)}) %all-gather.2.cloned.1.call-update) | async-done | bytes 1048592 | tf_op jit(solution)/shard_map/all_gather | solution.py:72
  734.2 2.1 reduce_sum.61
  736.3 229.6 %all-reduce.3.cloned.1.call-done = f32[128,256]{1,0:T(8,128)} async-done(((f32[128,256]{1,0:T(8,128)}), f32[128,256]{1,0:T(8,128)}) %all-reduce.3.cloned.1.call-update) | async-done | bytes 131088 | tf_op jit(solution)/shard_map/psum | solution.py:55
  965.9 1.6 copy.36
  967.4 0.0 copy-done.1
  (15 shorter events, 0.1 us)
Async XLA Ops:
  8.0 29.6 %copy-start = (bf16[1024,128]{1,0:T(8,128)(2,1)S(1)}, bf16[1024,128]{1,0:T(8,128)(2,1)}, u32[]{:S(2)}) copy-start(bf16[1024,128]{1,0:T(8,128)(2,1)} %param.6) | copy-start | bytes 786436
  46.2 191.0 %all-to-all-start.1 = ((bf16[128,2,128,128]{3,2,1,0:T(8,128)(2,1)}), bf16[128,2,128,128]{3,2,1,0:T(8,128)(2,1)}, u32[]{:S(2)}, u32[]{:S(2)}) async-start(bf16[128,2,128,128]{3,2,1,0:T(8,128)(2,1)} %bitcast.65), calls=%async_computation.1 | async-start | bytes 16777216 | tf_op jit(solution)/shard_map/all_to_all | solution.py:39
  249.2 17.1 %copy-start.2 = (bf16[128,256]{1,0:T(8,128)(2,1)S(1)}, bf16[128,256]{1,0:T(8,128)(2,1)}, u32[]{:S(2)}) copy-start(bf16[128,256]{1,0:T(8,128)(2,1)} %param.7) | copy-start | bytes 196612
  249.2 17.1 %copy-start.3 = (bf16[1024,256]{1,0:T(8,128)(2,1)S(1)}, bf16[1024,256]{1,0:T(8,128)(2,1)}, u32[]{:S(2)}) copy-start(bf16[1024,256]{1,0:T(8,128)(2,1)} %param.11) | copy-start | bytes 1572868
  314.6 372.8 %all-to-all-start.2 = ((f32[128,2,128,128]{3,2,1,0:T(8,128)}), f32[128,2,128,128]{3,2,1,0:T(8,128)}, u32[]{:S(2)}, u32[]{:S(2)}) async-start(f32[128,2,128,128]{3,2,1,0:T(8,128)} %bitcast.64), calls=%async_computation.2 | async-start | bytes 33554432 | tf_op jit(solution)/shard_map/all_to_all | solution.py:61
  322.4 411.8 %all-gather.2.cloned.1.call-start = ((), (), s32[]{:S(2)}) async-start(), calls=%async_computation.3 | async-start | bytes 1572864 | tf_op jit(solution)/shard_map/all_gather | solution.py:72
  687.3 280.1 %copy-start.1 = (bf16[1024,128]{1,0:T(8,128)(2,1)S(1)}, bf16[1024,128]{1,0:T(8,128)(2,1)}, u32[]{:S(2)}) copy-start(bf16[1024,128]{1,0:T(8,128)(2,1)} %param.6) | copy-start | bytes 786436
  708.1 257.8 %all-reduce.3.cloned.1.call-start = ((), (), s32[]{:S(2)}) async-start(), calls=%async_computation.4 | async-start | bytes 262144 | tf_op jit(solution)/shard_map/psum | solution.py:55
Sparse Core Ops, SparseCore 0:
  708.2 25.8 all-gather.1
Sparse Core Ops, SparseCore 1:
  714.7 251.1 all-reduce.2
